TPU v7x, 32 devices: a whole 2x2x4 slice. The times are simulated.
32 devices in a mesh: grp: 2 (over x), sfc: 16 (over z, y, core).
Axes of the slice: x: 2, y: 2, z: 4, core: 2. Of those that a mesh axis runs over, the one named last changes fastest.
Arguments:
- tracers: float32 [8, 64, 16384], P(None, None, ('grp', 'sfc')), parts along dimension 2, may hold values from -6 to 6
- velocity: float32 [2, 64, 16384], P(None, None, ('grp', 'sfc')), parts along dimension 2, may hold values from -4 to 4
- metric: float32 [16384], P(('grp', 'sfc')), parts along dimension 0, may hold values from 0.5 to 2
- absorber: bfloat16 [16384, 256], P(('grp', 'sfc')), parts along dimension 0, may hold values from 0.049804688 to 1
- cosine_zenith: bfloat16 [16384], P(('grp', 'sfc')), parts along dimension 0, may hold values from 0.049804688 to 1
- layer_mass: bfloat16 [64, 16384], P(None, ('grp', 'sfc')), parts along dimension 1, may hold values from 0.5 to 2
- absorption: bfloat16 [4, 112, 64], replicated, may hold values from 0.0009994507 to 0.29882812
- solar_flux: float32 [112], replicated, may hold values from 0.1 to 1
- sunlit: int32 [128], P(('grp', 'sfc')), parts along dimension 0, may hold values from 0 to 1, as said below
- neighbour: int32 [4, 1024], P(None, ('grp', 'sfc')), parts along dimension 1, may hold values from 0 to 511, as said below
- neighbour_edge: int32 [4, 1024], P(None, ('grp', 'sfc')), parts along dimension 1, may hold values from 0 to 3
Outputs:
- advanced: float32 [8, 64, 16384], P(None, None, ('grp', 'sfc')), parts along dimension 2
- heating: float32 [64, 16384], P(None, ('grp', 'sfc')), parts along dimension 1
There are 2 independent parts, one for each index of `grp`. A program takes and returns all parts, laid end to end along the dimension named above; an argument that names none is the same for every part. Nothing has to cross between parts.
Inputs may be any that keep to these rules, and one draw needn't show every extreme that they name: `sunlit`: the 1s form one cyclic run of 32 consecutive blocks; all other blocks are 0. For an element among the 32 elements of device position d along sfc (elements d * 32 to (d + 1) * 32 - 1), every neighbour lies among those elements or the 8 elements on either side of them, counted cyclically over 512; on every device both ends of that range are named.
All inputs are finite; a program needn't handle non-finite values.
Results may differ from a plain program's by a relative error of at most 0.0003.
Values may be sent and summed in bfloat16 or wider, within the bound.
No kernel may reach another device: no remote copies, remote signals or barrier semaphores. Data moves between devices by JAX's collectives and lax.ppermute only.
A program may use at most 64 MiB of HBM per device.

v0:
```python
import math

import jax
import jax.numpy as jnp
import numpy as np
from jax import lax
from jax.sharding import PartitionSpec as P

GPOINTS = 112
BLOCK_COLS = 128
RIM = 8


time_step = 0.1


def extended_2(value, sides, width):
    for axis, dim in sides:
        peers, length = (lax.axis_size(axis), value.shape[dim])
        up = [(i, (i + 1) % peers) for i in range(peers)]
        down = [(j, i) for i, j in up]
        last = lax.slice_in_dim(value, length - width, length, axis=dim)
        first = lax.slice_in_dim(value, 0, width, axis=dim)
        before = lax.ppermute(last, axis, up)
        after = lax.ppermute(first, axis, down)
        value = jnp.concatenate([before, value, after], axis=dim)
    return value


def derivative_table():
    gll_nodes = np.array([-1.0, -1.0 / math.sqrt(5.0), 1.0 / math.sqrt(5.0), 1.0])
    bary_weights = np.array(
        [
            1.0
            / np.prod(
                [gll_nodes[ipoint] - gll_nodes[mpoint] for mpoint in range(4) if mpoint != ipoint]
            )
            for ipoint in range(4)
        ]
    )
    deriv_table = np.zeros((4, 4))
    for ipoint in range(4):
        for mpoint in range(4):
            if ipoint != mpoint:
                deriv_table[ipoint, mpoint] = (
                    bary_weights[mpoint]
                    / bary_weights[ipoint]
                    / (gll_nodes[ipoint] - gll_nodes[mpoint])
                )
        deriv_table[ipoint, ipoint] = -sum(
            (deriv_table[ipoint, mpoint] for mpoint in range(4) if mpoint != ipoint)
        )
    return deriv_table


def as_points(field):
    return field.reshape(field.shape[:-1] + (-1, 4, 4))


def tendency(state_field, velocity, metric, deriv_table):
    first_axis = jnp.stack(
        [
            sum(
                (
                    float(deriv_table[ipoint, mpoint]) * state_field[:, :, :, mpoint, :]
                    for mpoint in range(4)
                )
            )
            for ipoint in range(4)
        ],
        axis=3,
    )
    second_axis = jnp.stack(
        [
            sum(
                (
                    float(deriv_table[jpoint, mpoint]) * state_field[:, :, :, :, mpoint]
                    for mpoint in range(4)
                )
            )
            for jpoint in range(4)
        ],
        axis=4,
    )
    return -(velocity[0] * first_axis + velocity[1] * second_axis) * metric


def edge_values(state_field):
    return jnp.stack(
        [
            state_field[:, :, :, 0, :],
            state_field[:, :, :, :, 3],
            state_field[:, :, :, 3, ::-1],
            state_field[:, :, :, ::-1, 0],
        ],
        axis=3,
    )


def apply_edges(state_field, change):
    state_field = state_field.at[:, :, :, 0, :].add(change[:, :, :, 0, :])
    state_field = state_field.at[:, :, :, :, 3].add(change[:, :, :, 1, :])
    state_field = state_field.at[:, :, :, 3, :].add(change[:, :, :, 2, ::-1])
    state_field = state_field.at[:, :, :, :, 0].add(change[:, :, :, 3, ::-1])
    return state_field


def shards(
    tracers,
    velocity,
    metric,
    absorber,
    cosine_zenith,
    layer_mass,
    absorption,
    solar_flux,
    sunlit,
    neighbour,
    neighbour_edge,
):
    deriv_table = derivative_table()
    devices = lax.axis_size("sfc")
    position = lax.axis_index("sfc")
    tracer_pts = as_points(tracers)
    wind_pts = as_points(velocity)
    metric_pts = as_points(metric)
    local_elems = tracer_pts.shape[2]
    extended = local_elems + 2 * RIM
    total_elems = local_elems * devices
    local_index = (neighbour - position * local_elems + RIM) % total_elems
    facing_index = (local_index * 4 + neighbour_edge).T.reshape(-1)

    def stiffness(state_field):
        edge_vals = edge_values(state_field)
        padded = extended_2(edge_vals, (("sfc", 2),), RIM)
        flattened = padded[:, :, :, :, ::-1].reshape(
            state_field.shape[0], state_field.shape[1], 4 * extended, 4
        )
        facing = jnp.take(flattened, facing_index, axis=2).reshape(edge_vals.shape)
        return apply_edges(state_field, 0.5 * (facing - edge_vals))

    first_section = stiffness(
        tracer_pts + time_step * tendency(tracer_pts, wind_pts, metric_pts, deriv_table)
    )
    levels = layer_mass.shape[0]
    blocks_dev = sunlit.shape[0]
    absorb_blocks = absorber.reshape(blocks_dev, BLOCK_COLS, -1)
    cosine_blocks = cosine_zenith.reshape(blocks_dev, BLOCK_COLS)
    mass_blocks = layer_mass.reshape(levels, blocks_dev, BLOCK_COLS).transpose(1, 0, 2)
    triangle = (jnp.arange(levels)[:, None] <= jnp.arange(levels)[None, :]).astype(jnp.bfloat16)
    big_weights = (
        (absorption[:, :, :, None] * triangle[None, None, :, :])
        .transpose(0, 2, 1, 3)
        .reshape(absorption.shape[0] * levels, GPOINTS * levels)
    )
    flux_top = jnp.sum(solar_flux)

    def column_heating(pieces):
        amounts, cosines, masses = pieces
        optical_path = jnp.dot(amounts, big_weights, preferred_element_type=jnp.float32).reshape(
            amounts.shape[0], GPOINTS, levels
        )
        slant_cos = cosines.astype(jnp.float32)
        transmit = jnp.exp(-optical_path / slant_cos[:, None, None])
        downward = jnp.einsum("cgl,g->cl", transmit, solar_flux, precision=lax.Precision.HIGHEST)
        flux_above = jnp.concatenate(
            [jnp.broadcast_to(flux_top, (downward.shape[0], 1)), downward[:, :-1]], axis=1
        )
        return (slant_cos[:, None] * (flux_above - downward)).T / masses.astype(jnp.float32)

    def maybe_heating(pieces):
        amounts, cosines, masses, lit_flag = pieces
        return lax.cond(
            lit_flag > 0,
            column_heating,
            lambda unused: jnp.zeros((levels, BLOCK_COLS), jnp.float32),
            (amounts, cosines, masses),
        )

    heat_blocks = lax.map(maybe_heating, (absorb_blocks, cosine_blocks, mass_blocks, sunlit))
    heating = heat_blocks.transpose(1, 0, 2).reshape(levels, -1)
    forcing = as_points(heating)
    section_tendency = tendency(first_section, wind_pts, metric_pts, deriv_table).at[0].add(forcing)
    advanced = stiffness(0.5 * tracer_pts + 0.5 * (first_section + time_step * section_tendency))
    return (advanced.reshape(tracers.shape), heating)


def solution(mesh):
    placed = (
        P(None, None, ("grp", "sfc")),
        P(None, None, ("grp", "sfc")),
        P(("grp", "sfc")),
        P(("grp", "sfc"), None),
        P(("grp", "sfc")),
        P(None, ("grp", "sfc")),
        P(),
        P(),
        P(("grp", "sfc")),
        P(None, ("grp", "sfc")),
        P(None, ("grp", "sfc")),
    )
    return jax.shard_map(
        shards,
        mesh=mesh,
        in_specs=placed,
        out_specs=(P(None, None, ("grp", "sfc")), P(None, ("grp", "sfc"))),
        check_vma=False,
    )
```

profile of v0, /device:TPU:9, one launch (start us, length us, event | category | flops | bytes accessed | tf_op | source)
XLA Modules:
  0.0 203.2 jit_solution(10580495202348531570)
XLA Ops:
  6.6 3.5 %fusion.20 = f32[8,64,32,4,4]{1,0,4,3,2:T(8,128)S(1)} fusion(f32[8,64,32,4,4]{1,0,4,3,2:T(8,128)S(1)} %bitcast.102, f32[8,64,32,1,4]{1,0,4,3,2:T(8,128)} %get-tuple-element.351, f32[8,64,32,1,4]{1,0,4,3,2:T(8,128)} %get-tuple-element.350, f32[8,64,32,1,4]{1,0,4,3,2:T(8,128)} %get-tuple-element.349, f32[8,64,32,1,4]{1,0,4,3,2:T(8,128)S(1)} %get-tuple-element.348, ...), kind=kLoop, calls=%fused_computation.28 | loop fusion | flops 3407872 | bytes 4458496 | tf_op jit(solution)/shard_map/add | solution.py:143
  15.6 129.9 %while.20 = (s32[]{:T(128)}, f32[4,64,128]{2,1,0:T(8,128)S(1)}, s32[4]{0:T(128)S(1)}, bf16[4,128]{1,0:T(4,128)(2,1)S(1)}, bf16[4,128,256]{2,1,0:T(8,128)(2,1)}, ...) while((s32[]{:T(128)}, f32[4,64,128]{2,1,0:T(8,128)S(1)}, ...), condition=%wide.region_4.6_spmd.clone, body=%wide.region_1.5_spmd.clone.sunk | while | flops 484475008 | bytes 29706672 | solution.py:180
  16.8 31.2 %conditional.3 = (f32[1,64,128]{2,1,0:T(8,128)S(1)}) conditional(s32[]{:T(128)} %bitcast.96, () %tuple.108, (bf16[4,128]{1,0:T(4,128)(2,1)S(1)}, s32[]{:T(128)}, bf16[4,128,256]{2,1,0:T(8,128)(2,1)}, bf16[4,64,112]{2,1,0:T(8,128)(2,1)S(1)}, f32[112]{0:T(128)S(1)}, /*index=5*/f32[]{:T(128)}, bf16[4,64,128]{2,1,0:T(8,128)(2,1)S(1)}, ...), branch_computations={%region_2.3_spmd, %region_3.4_spmd} | conditional | flops 484475008 | bytes 29640916 | solution.py:173
  16.8 6.5 %broadcast_multiply_fusion = bf16[4,64,112,64]{3,2,1,0:T(8,128)(2,1)} fusion(bf16[64,64]{1,0:T(8,128)(2,1)S(1)} %get-tuple-element.295, bf16[4,64,112]{2,1,0:T(8,128)(2,1)S(1)} %get-tuple-element.294), kind=kLoop, calls=%fused_computation.3 | loop fusion | flops 1835008 | bytes 3735552 | tf_op jit(solution)/shard_map/mul | solution.py:152
  23.4 9.4 %mul.466 = bf16[256,7168]{1,0:T(8,128)(2,1)} reshape(bf16[4,64,112,64]{3,2,1,0:T(8,128)(2,1)} %broadcast_multiply_fusion) | data formatting | bytes 7340032 | tf_op jit(solution)/shard_map/mul | solution.py:152
  32.8 5.9 %copy.61 = bf16[256,7168]{0,1:T(8,128)(2,1)} copy(bf16[256,7168]{1,0:T(8,128)(2,1)} %mul.466) | data formatting | bytes 7340032 | tf_op jit(solution)/shard_map
  38.7 6.2 %fusion.2 = f32[128,112,64]{0,1,2:T(8,128)S(1)} fusion(bf16[112,64,256]{2,1,0:T(8,128)(2,1)} %bitcast.99, bf16[4,128,256]{2,1,0:T(8,128)(2,1)} %get-tuple-element.210, s32[]{:T(128)} %get-tuple-element.209), kind=kOutput, calls=%fused_computation.4 | convolution fusion | flops 469762048 | bytes 7406080 | tf_op jit(solution)/shard_map/while/body/eval_jaxpr/cond/branch_1_fun/dot_general | solution.py:160
  49.3 31.2 %conditional.3 = (f32[1,64,128]{2,1,0:T(8,128)S(1)}) conditional(s32[]{:T(128)} %bitcast.96, () %tuple.108, (bf16[4,128]{1,0:T(4,128)(2,1)S(1)}, s32[]{:T(128)}, bf16[4,128,256]{2,1,0:T(8,128)(2,1)}, bf16[4,64,112]{2,1,0:T(8,128)(2,1)S(1)}, f32[112]{0:T(128)S(1)}, /*index=5*/f32[]{:T(128)}, bf16[4,64,128]{2,1,0:T(8,128)(2,1)S(1)}, ...), branch_computations={%region_2.3_spmd, %region_3.4_spmd} | conditional | flops 484475008 | bytes 29640916 | solution.py:173
  49.3 6.5 %broadcast_multiply_fusion = bf16[4,64,112,64]{3,2,1,0:T(8,128)(2,1)} fusion(bf16[64,64]{1,0:T(8,128)(2,1)S(1)} %get-tuple-element.295, bf16[4,64,112]{2,1,0:T(8,128)(2,1)S(1)} %get-tuple-element.294), kind=kLoop, calls=%fused_computation.3 | loop fusion | flops 1835008 | bytes 3735552 | tf_op jit(solution)/shard_map/mul | solution.py:152
  55.8 9.4 %mul.466 = bf16[256,7168]{1,0:T(8,128)(2,1)} reshape(bf16[4,64,112,64]{3,2,1,0:T(8,128)(2,1)} %broadcast_multiply_fusion) | data formatting | bytes 7340032 | tf_op jit(solution)/shard_map/mul | solution.py:152
  65.3 5.9 %copy.61 = bf16[256,7168]{0,1:T(8,128)(2,1)} copy(bf16[256,7168]{1,0:T(8,128)(2,1)} %mul.466) | data formatting | bytes 7340032 | tf_op jit(solution)/shard_map
  71.2 6.2 %fusion.2 = f32[128,112,64]{0,1,2:T(8,128)S(1)} fusion(bf16[112,64,256]{2,1,0:T(8,128)(2,1)} %bitcast.99, bf16[4,128,256]{2,1,0:T(8,128)(2,1)} %get-tuple-element.210, s32[]{:T(128)} %get-tuple-element.209), kind=kOutput, calls=%fused_computation.4 | convolution fusion | flops 469762048 | bytes 7406080 | tf_op jit(solution)/shard_map/while/body/eval_jaxpr/cond/branch_1_fun/dot_general | solution.py:160
  81.7 31.2 %conditional.3 = (f32[1,64,128]{2,1,0:T(8,128)S(1)}) conditional(s32[]{:T(128)} %bitcast.96, () %tuple.108, (bf16[4,128]{1,0:T(4,128)(2,1)S(1)}, s32[]{:T(128)}, bf16[4,128,256]{2,1,0:T(8,128)(2,1)}, bf16[4,64,112]{2,1,0:T(8,128)(2,1)S(1)}, f32[112]{0:T(128)S(1)}, /*index=5*/f32[]{:T(128)}, bf16[4,64,128]{2,1,0:T(8,128)(2,1)S(1)}, ...), branch_computations={%region_2.3_spmd, %region_3.4_spmd} | conditional | flops 484475008 | bytes 29640916 | solution.py:173
  81.8 6.5 %broadcast_multiply_fusion = bf16[4,64,112,64]{3,2,1,0:T(8,128)(2,1)} fusion(bf16[64,64]{1,0:T(8,128)(2,1)S(1)} %get-tuple-element.295, bf16[4,64,112]{2,1,0:T(8,128)(2,1)S(1)} %get-tuple-element.294), kind=kLoop, calls=%fused_computation.3 | loop fusion | flops 1835008 | bytes 3735552 | tf_op jit(solution)/shard_map/mul | solution.py:152
  88.3 9.4 %mul.466 = bf16[256,7168]{1,0:T(8,128)(2,1)} reshape(bf16[4,64,112,64]{3,2,1,0:T(8,128)(2,1)} %broadcast_multiply_fusion) | data formatting | bytes 7340032 | tf_op jit(solution)/shard_map/mul | solution.py:152
  97.7 5.9 %copy.61 = bf16[256,7168]{0,1:T(8,128)(2,1)} copy(bf16[256,7168]{1,0:T(8,128)(2,1)} %mul.466) | data formatting | bytes 7340032 | tf_op jit(solution)/shard_map
  103.7 6.2 %fusion.2 = f32[128,112,64]{0,1,2:T(8,128)S(1)} fusion(bf16[112,64,256]{2,1,0:T(8,128)(2,1)} %bitcast.99, bf16[4,128,256]{2,1,0:T(8,128)(2,1)} %get-tuple-element.210, s32[]{:T(128)} %get-tuple-element.209), kind=kOutput, calls=%fused_computation.4 | convolution fusion | flops 469762048 | bytes 7406080 | tf_op jit(solution)/shard_map/while/body/eval_jaxpr/cond/branch_1_fun/dot_general | solution.py:160
  114.2 31.2 %conditional.3 = (f32[1,64,128]{2,1,0:T(8,128)S(1)}) conditional(s32[]{:T(128)} %bitcast.96, () %tuple.108, (bf16[4,128]{1,0:T(4,128)(2,1)S(1)}, s32[]{:T(128)}, bf16[4,128,256]{2,1,0:T(8,128)(2,1)}, bf16[4,64,112]{2,1,0:T(8,128)(2,1)S(1)}, f32[112]{0:T(128)S(1)}, /*index=5*/f32[]{:T(128)}, bf16[4,64,128]{2,1,0:T(8,128)(2,1)S(1)}, ...), branch_computations={%region_2.3_spmd, %region_3.4_spmd} | conditional | flops 484475008 | bytes 29640916 | solution.py:173
  114.2 6.5 %broadcast_multiply_fusion = bf16[4,64,112,64]{3,2,1,0:T(8,128)(2,1)} fusion(bf16[64,64]{1,0:T(8,128)(2,1)S(1)} %get-tuple-element.295, bf16[4,64,112]{2,1,0:T(8,128)(2,1)S(1)} %get-tuple-element.294), kind=kLoop, calls=%fused_computation.3 | loop fusion | flops 1835008 | bytes 3735552 | tf_op jit(solution)/shard_map/mul | solution.py:152
  120.8 9.4 %mul.466 = bf16[256,7168]{1,0:T(8,128)(2,1)} reshape(bf16[4,64,112,64]{3,2,1,0:T(8,128)(2,1)} %broadcast_multiply_fusion) | data formatting | bytes 7340032 | tf_op jit(solution)/shard_map/mul | solution.py:152
  130.2 5.9 %copy.61 = bf16[256,7168]{0,1:T(8,128)(2,1)} copy(bf16[256,7168]{1,0:T(8,128)(2,1)} %mul.466) | data formatting | bytes 7340032 | tf_op jit(solution)/shard_map
  136.1 6.2 %fusion.2 = f32[128,112,64]{0,1,2:T(8,128)S(1)} fusion(bf16[112,64,256]{2,1,0:T(8,128)(2,1)} %bitcast.99, bf16[4,128,256]{2,1,0:T(8,128)(2,1)} %get-tuple-element.210, s32[]{:T(128)} %get-tuple-element.209), kind=kOutput, calls=%fused_computation.4 | convolution fusion | flops 469762048 | bytes 7406080 | tf_op jit(solution)/shard_map/while/body/eval_jaxpr/cond/branch_1_fun/dot_general | solution.py:160
  161.3 7.9 %scatter-add.36 = f32[8,64,32,4,4]{1,0,4,3,2:T(8,128)} dynamic-update-slice(f32[8,64,32,4,4]{1,0,4,3,2:T(8,128)} %copy-done.5, f32[1,64,32,4,4]{1,0,4,3,2:T(1,128)S(1)} %slice_add_fusion.6, s32[]{:T(128)} %constant.304.clone.1, s32[]{:T(128)} %constant.304.clone.1, s32[]{:T(128)} %constant.304.clone.1, s32[]{:T(128)} %constant.304.clone.1, s32[]{:T(128)} %constant.304.clone.1) | dynamic-update-slice | bytes 262148 | tf_op jit(solution)/shard_map/scatter-add | solution.py:183
  177.3 11.0 %collective-permute-done.2 = f32[8,64,8,4,4]{1,0,4,3,2:T(8,128)S(1)} collective-permute-done((f32[8,64,8,4,4]{1,0,4,3,2:T(8,128)S(1)}, f32[8,64,8,4,4]{1,0,4,3,2:T(8,128)S(1)}, u32[]{:S(2)}, u32[]{:S(2)}) %collective-permute-start.2) | collective-permute-done | bytes 262176 | tf_op jit(solution)/shard_map/ppermute | solution.py:24
  (157 shorter events, 64.7 us)
Async XLA Ops:
  2.6 3.9 %copy-start.2 = (f32[8,64,512]{1,0,2:T(8,128)}, f32[8,64,512]{1,0,2:T(8,128)S(1)}, u32[]{:S(2)}) copy-start(f32[8,64,512]{1,0,2:T(8,128)S(1)} %copy.62) | copy-start | bytes 3145732
  4.5 1.6 copy-start.31
  4.5 1.8 copy-start.29
  6.4 3.7 %copy-start.22 = (f32[1,64,512]{1,2,0:T(8,128)}, f32[1,64,512]{1,2,0:T(8,128)S(1)}, u32[]{:S(2)}) copy-start(f32[1,64,512]{1,2,0:T(8,128)S(1)} %copy.89) | copy-start | bytes 393220
  6.6 3.5 %copy-start.24 = (f32[1,64,512]{1,2,0:T(8,128)}, f32[1,64,512]{1,2,0:T(8,128)S(1)}, u32[]{:S(2)}) copy-start(f32[1,64,512]{1,2,0:T(8,128)S(1)} %copy.90) | copy-start | bytes 393220
  12.6 2.0 copy-start.32
  12.6 2.0 %copy-start.33 = (s32[4,32]{1,0:T(4,128)S(1)}, s32[4,32]{1,0:T(4,128)}, u32[]{:S(2)}) copy-start(s32[4,32]{1,0:T(4,128)} %param.44) | copy-start | bytes 1540
  12.6 2.3 %copy-start.30 = (bf16[64,512]{1,0:T(8,128)(2,1)S(1)}, bf16[64,512]{1,0:T(8,128)(2,1)}, u32[]{:S(2)}) copy-start(bf16[64,512]{1,0:T(8,128)(2,1)} %param.40) | copy-start | bytes 196612
  12.6 2.3 %copy-start.36 = (f32[112]{0:T(128)S(1)}, f32[112]{0:T(128)}, u32[]{:S(2)}) copy-start(f32[112]{0:T(128)} %param.42) | copy-start | bytes 1348
  12.6 3.0 %copy-start.26 = (bf16[4,112,64]{1,2,0:T(8,128)(2,1)S(1)}, bf16[4,112,64]{1,2,0:T(8,128)(2,1)}, u32[]{:S(2)}) copy-start(bf16[4,112,64]{1,2,0:T(8,128)(2,1)} %param.41) | copy-start | bytes 172036
  12.6 3.0 %copy-start.34 = (bf16[512]{0:T(512)(128)(2,1)S(1)}, bf16[512]{0:T(512)(128)(2,1)}, u32[]{:S(2)}) copy-start(bf16[512]{0:T(512)(128)(2,1)} %param.39) | copy-start | bytes 3076
  12.6 3.0 %copy-start.35 = (s32[4]{0:T(128)S(1)}, s32[4]{0:T(128)}, u32[]{:S(2)}) copy-start(s32[4]{0:T(128)} %param.43) | copy-start | bytes 52
  12.7 132.9 %collective-permute-start = (f32[8,64,8,4,4]{1,0,4,3,2:T(8,128)S(1)}, f32[8,64,8,4,4]{1,0,4,3,2:T(8,128)S(1)}, u32[]{:S(2)}, u32[]{:S(2)}) collective-permute-start(f32[8,64,8,4,4]{1,0,4,3,2:T(8,128)S(1)} %get-tuple-element.338), channel_id=1, source_target_pairs={{0,1},{1,2},{2,3},{3,4},{4,5},{5,6},{6,7},{7,8},{8,9},{9,10},{10,1... | collective-permute-start | bytes 786440 | tf_op jit(solution)/shard_map/ppermute | solution.py:24
  14.6 131.9 %collective-permute-start.1 = (f32[8,64,8,4,4]{1,0,4,3,2:T(8,128)S(1)}, f32[8,64,8,4,4]{1,0,4,3,2:T(8,128)}, u32[]{:S(2)}, u32[]{:S(2)}) collective-permute-start(f32[8,64,8,4,4]{1,0,4,3,2:T(8,128)S(1)} %get-tuple-element.339), channel_id=1, source_target_pairs={{1,0},{2,1},{3,2},{4,3},{5,4},{6,5},{7,6},{8,7},{9,8},{10,9},{11,1... | collective-permute-start | bytes 786440 | tf_op jit(solution)/shard_map/ppermute | solution.py:25
  153.3 1.3 copy-start.15
  153.3 1.5 copy-start.17
  154.8 1.6 copy-start.1
  172.2 1.3 copy-start.3
  172.3 1.4 copy-start.18
  174.8 13.5 %collective-permute-start.2 = (f32[8,64,8,4,4]{1,0,4,3,2:T(8,128)S(1)}, f32[8,64,8,4,4]{1,0,4,3,2:T(8,128)S(1)}, u32[]{:S(2)}, u32[]{:S(2)}) collective-permute-start(f32[8,64,8,4,4]{1,0,4,3,2:T(8,128)S(1)} %get-tuple-element.325), channel_id=1, source_target_pairs={{0,1},{1,2},{2,3},{3,4},{4,5},{5,6},{6,7},{7,8},{8,9},{9,10},{10,1... | collective-permute-start | bytes 786440 | tf_op jit(solution)/shard_map/ppermute | solution.py:24
  176.5 14.3 %collective-permute-start.3 = (f32[8,64,8,4,4]{1,0,4,3,2:T(8,128)S(1)}, f32[8,64,8,4,4]{1,0,4,3,2:T(8,128)}, u32[]{:S(2)}, u32[]{:S(2)}) collective-permute-start(f32[8,64,8,4,4]{1,0,4,3,2:T(8,128)S(1)} %get-tuple-element.326), channel_id=1, source_target_pairs={{1,0},{2,1},{3,2},{4,3},{5,4},{6,5},{7,6},{8,7},{9,8},{10,9},{11,1... | collective-permute-start | bytes 786440 | tf_op jit(solution)/shard_map/ppermute | solution.py:25
  197.8 1.3 copy-start.19
  197.8 1.5 copy-start.21
  199.3 1.6 copy-start.4
  (17 other events, 17.8 us)
where the time goes:
time: 206 us; the launch traced here: 203 us
  local copies, waits for them, and re-layouts  98.5 us (48%)
  other arithmetic  49.9 us (24%)
  matrix products  34.5 us (17%)
  waiting for transfers between devices  12.7 us (6%)
  starting transfers between devices  3.65 us (2%)
  loops' own time  2.67 us (1%)
    mul x4, local copies, waits for them, and re-layouts, shards(): absorption[:, :, :, None] * triangle[None, None, :, :]  37.7 us
    mul x4, other arithmetic, shards(): absorption[:, :, :, None] * triangle[None, None, :, :]  26.2 us
    dot_general x4, matrix products, column_heating(): jnp.dot(amounts, big_weights, preferred_element_type=jnp.float32)  24.7 us
    another operation x6, local copies, waits for them, and re-layouts  23.8 us
    unnamed x80, local copies, waits for them, and re-layouts  16.5 us
    ppermute x2, waiting for transfers between devices, extended_2(): before = lax.ppermute(last, axis, up)  11 us
    dot_general x4, matrix products, column_heating(): jnp.einsum('cgl,g->cl', transmit, solar_flux, precision=lax.Precision.HIG...  9.83 us
    scatter-add x1, local copies, waits for them, and re-layouts, shards(): tendency(first_section, wind_pts, metric_pts, deriv_table).at[0]  7.9 us
  transfers between devices with their start and end apart: 4, of which 2 were waited for; matrix products, arithmetic and copies ran while one was open for 63% of the time, Pallas kernels for 0%

commit v1 on v0

v1 whole, which is shorter than its diff:
```python
import functools
import math

import jax
import jax.numpy as jnp
import numpy as np
from jax import lax
from jax.experimental import pallas as pl
from jax.experimental.pallas import tpu as pltpu
from jax.sharding import PartitionSpec as P

BLOCK = 128
RIM = 8
STEP = 0.1
F32 = jnp.float32
BF16 = jnp.bfloat16
VMEM = pl.BlockSpec(memory_space=pltpu.VMEM)
SMEM = pl.BlockSpec(memory_space=pltpu.SMEM)
HBM = pl.BlockSpec(memory_space=pl.ANY)


def derivative_table():
    nodes = np.array([-1.0, -1.0 / math.sqrt(5.0), 1.0 / math.sqrt(5.0), 1.0])
    weights = np.array(
        [1.0 / np.prod([nodes[i] - nodes[m] for m in range(4) if m != i]) for i in range(4)]
    )
    table = np.zeros((4, 4))
    for i in range(4):
        for m in range(4):
            if i != m:
                table[i, m] = weights[m] / weights[i] / (nodes[i] - nodes[m])
        table[i, i] = -sum(table[i, m] for m in range(4) if m != i)
    return table


def params(mib=8):
    return pltpu.CompilerParams(vmem_limit_bytes=mib << 20)


def cost(flops, size=1 << 20):
    return pl.CostEstimate(flops=int(flops), bytes_accessed=int(size), transcendentals=0)


def iota(shape, dim):
    return lax.broadcasted_iota(jnp.int32, shape, dim)


def split(x):
    high = x.astype(BF16)
    return high, (x - high.astype(F32)).astype(BF16)


def dot(a, b):
    return jnp.dot(a, b, preferred_element_type=F32)


def build_derivatives(wide_ref, fine_ref):
    table = derivative_table()
    src, dst = iota((BLOCK, BLOCK), 0), iota((BLOCK, BLOCK), 1)
    si, sj, di, dj = src // 4 % 4, src % 4, dst // 4 % 4, dst % 4
    same = src // 16 == dst // 16
    halves = []
    for d, s, keep in ((di, si, same & (sj == dj)), (dj, sj, same & (si == di))):
        pick = jnp.where(keep, d * 4 + s, -1)
        value = jnp.zeros((BLOCK, BLOCK), F32)
        for i in range(4):
            for m in range(4):
                value = jnp.where(pick == i * 4 + m, float(table[i, m]), value)
        halves.append(value)
    high, low = split(jnp.concatenate(halves, axis=1))
    wide_ref[:BLOCK] = high
    wide_ref[BLOCK:] = high
    fine_ref[...] = low


def advance(field, first, second, wide_ref, fine_ref):
    high, low = split(field)
    both = dot(jnp.concatenate([high, low], axis=1), wide_ref[...]) + dot(high, fine_ref[...])
    return field + first * both[:, :BLOCK] + second * both[:, BLOCK:]


def repeat_rows(x, times):
    return jnp.concatenate([x] * times, axis=0) if times > 1 else x


def rim_kernel(levels, tr_hbm, vel_hbm, metric, left, right, wide, fine, tr, vel, sems):
    cols = metric.shape[1]
    starts = (0, cols - BLOCK)
    copies = []
    for r, c0 in enumerate(starts):
        copies.append(pltpu.make_async_copy(vel_hbm.at[:, pl.ds(c0, BLOCK)], vel.at[r], sems.at[r]))
        copies.append(pltpu.make_async_copy(tr_hbm.at[:, pl.ds(c0, BLOCK)], tr.at[r], sems.at[2 + r]))
    for copy in copies:
        copy.start()
    build_derivatives(wide, fine)
    for copy in copies:
        copy.wait()
    rows = tr.shape[1]
    for r, out in enumerate((left, right)):
        scale = -STEP * metric[:, pl.ds(starts[r], BLOCK)]
        first = repeat_rows(vel[r, :levels] * scale, rows // levels)
        second = repeat_rows(vel[r, levels:] * scale, rows // levels)
        out[...] = advance(tr[r], first, second, wide, fine)


def build_assembly(total, position, nb, ne, local, halo):
    elems, cols = nb.shape[1], local.shape[1]
    index = nb[...] - position * elems + RIM
    index = jnp.where(index < 0, index + total, index)
    index = jnp.where(index >= total, index - total, index)
    code = (index * 4 + ne[...]).astype(F32).astype(BF16)
    spread = (iota((elems, cols), 1) // 16 == iota((elems, cols), 0)).astype(F32).astype(BF16)
    code = dot(code, spread).astype(jnp.int32)
    lane = iota((1, cols), 1)
    i, j = lane // 4 % 4, lane % 4

    def source(code, p):
        edge, q = code % 4, 3 - p
        si = jnp.where(edge == 0, 0, jnp.where(edge == 1, q, jnp.where(edge == 2, 3, 3 - q)))
        sj = jnp.where(edge == 0, q, jnp.where(edge == 1, 3, jnp.where(edge == 2, 3 - q, 0)))
        return code // 4 * 16 + si * 4 + sj

    across = jnp.where(i == 0, source(code[0:1], j), source(code[2:3], 3 - j))
    across = jnp.where((i == 0) | (i == 3), across, -1)
    along = jnp.where(j == 3, source(code[1:2], i), source(code[3:4], 3 - i))
    along = jnp.where((j == 0) | (j == 3), along, -1)
    own = 1.0 - 0.5 * ((across >= 0).astype(F32) + (along >= 0).astype(F32))

    def rows_of(start):
        row = iota((BLOCK, cols), 0) + start
        return jnp.where(row == across, 0.5, 0.0) + jnp.where(row == along, 0.5, 0.0)

    halo[:BLOCK] = rows_of(0).astype(BF16)
    halo[BLOCK:] = rows_of(BLOCK + cols).astype(BF16)
    for r in range(0, cols, BLOCK):
        value = rows_of(BLOCK + r) + jnp.where(iota((BLOCK, cols), 0) + r == lane, own, 0.0)
        local[r : r + BLOCK] = value.astype(BF16)


def first_kernel(
    total, levels, chunk, tr, vel, metric, wide, fine, left, right, nb, ne, part, speed, local, halo
):
    rows, cols = tr.shape
    scale = -STEP * metric[...]
    speed[...] = vel[...] * scale
    build_assembly(total, lax.axis_index("sfc"), nb, ne, local, halo)

    def body(c, carry):
        r = pl.ds(pl.multiple_of(c * chunk, chunk), chunk)
        tiles = [left[r]]
        for b in range(BLOCK, cols - BLOCK, BLOCK):
            first = repeat_rows(speed[:levels, b : b + BLOCK], chunk // levels)
            second = repeat_rows(speed[levels:, b : b + BLOCK], chunk // levels)
            tiles.append(advance(tr[r, b : b + BLOCK], first, second, wide, fine))
        tiles.append(right[r])
        high, low = split(jnp.concatenate(tiles, axis=1))
        part[r] = dot(high, local[...]) + dot(low, local[...])
        return carry

    lax.fori_loop(0, rows // chunk, body, 0)


def halo_parts(left, right):
    lh, ll = split(left)
    rh, rl = split(right)
    return jnp.concatenate([lh, rh], axis=1), jnp.concatenate([ll, rl], axis=1)


def rim2_kernel(levels, part, left, right, halo, wide, fine, tr, speed, heat, out_left, out_right):
    rows, cols = part.shape
    high, low = halo_parts(left[...], right[...])
    for r, (c0, out) in enumerate(((0, out_left), (cols - BLOCK, out_right))):
        tile = pl.ds(c0, BLOCK)
        section = part[:, tile] + dot(high, halo[:, tile]) + dot(low, halo[:, tile])
        first = repeat_rows(speed[:levels, tile], rows // levels)
        second = repeat_rows(speed[levels:, tile], rows // levels)
        out[...] = 0.5 * (tr[:, tile] + advance(section, first, second, wide, fine))
        out[:levels] += (0.5 * STEP) * heat[:, r * BLOCK : (r + 1) * BLOCK]


def inner2_kernel(
    levels, chunk, part, left, right, halo, local, wide, fine, tr, speed, heat_rim, heat_in,
    own_left, own_right, out, heating,
):
    rows, cols = part.shape
    heating[:, :BLOCK] = heat_rim[:, :BLOCK]
    heating[:, BLOCK : cols - BLOCK] = heat_in[...]
    heating[:, cols - BLOCK :] = heat_rim[:, BLOCK:]

    def body(c, carry):
        r = pl.ds(pl.multiple_of(c * chunk, chunk), chunk)
        high, low = halo_parts(left[r], right[r])
        inner = halo[:, BLOCK : cols - BLOCK]
        section = part[r, BLOCK : cols - BLOCK] + dot(high, inner) + dot(low, inner)
        tiles = [own_left[r]]
        warm = jnp.where(c == 0, 0.5 * STEP, 0.0)
        for b in range(BLOCK, cols - BLOCK, BLOCK):
            first = repeat_rows(speed[:levels, b : b + BLOCK], chunk // levels)
            second = repeat_rows(speed[levels:, b : b + BLOCK], chunk // levels)
            field = advance(section[:, b - BLOCK : b], first, second, wide, fine)
            field = 0.5 * (tr[r, b : b + BLOCK] + field)
            add = warm * heat_in[:, b - BLOCK : b]
            if chunk > levels:
                add = jnp.concatenate([add, jnp.zeros((chunk - levels, BLOCK), F32)], axis=0)
            tiles.append(field + add)
        tiles.append(own_right[r])
        high, low = split(jnp.concatenate(tiles, axis=1))
        out[r] = dot(high, local[...]) + dot(low, local[...])
        return carry

    lax.fori_loop(0, rows // chunk, body, 0)


def last_kernel(chunk, part, left, right, halo, out):
    def body(c, carry):
        r = pl.ds(pl.multiple_of(c * chunk, chunk), chunk)
        high, low = halo_parts(left[r], right[r])
        out[r] = part[r] + dot(high, halo[...]) + dot(low, halo[...])
        return carry

    lax.fori_loop(0, part.shape[0] // chunk, body, 0)


def heat_kernel(
    blocks, group, absorber, cosine, mass, absorption, flux, lit, out, table, depth
):
    gases, points, levels = absorption.shape
    width = len(blocks) * BLOCK
    any_lit = lit[blocks[0]]
    for b in blocks[1:]:
        any_lit = any_lit + lit[b]

    @pl.when(any_lit == 0)
    def _():
        out[...] = jnp.zeros_like(out)

    @pl.when(any_lit > 0)
    def _():
        table[...] = jnp.concatenate([absorption[s].astype(F32) for s in range(gases)], axis=1)
        amounts = jnp.concatenate([absorber[b * BLOCK : (b + 1) * BLOCK] for b in blocks], axis=0)
        cos = jnp.concatenate([cosine[:, b * BLOCK : (b + 1) * BLOCK] for b in blocks], axis=1)
        cos = cos.astype(F32)
        scale = -math.log2(math.e) / cos
        shape = (levels, gases * levels)
        keep = iota(shape, 1) % levels <= iota(shape, 0)

        def body(c, carry):
            down, top = carry
            rows = []
            for k in range(group):
                row = table[pl.ds(c * group + k, 1), :]
                rows.append(jnp.where(keep, row, 0.0).astype(BF16))
            weights = jnp.concatenate(rows, axis=0)
            depth[...] = lax.dot_general(
                weights, amounts, (((1,), (1,)), ((), ())), preferred_element_type=F32
            )
            for k in range(group):
                f = flux[c * group + k]
                down = down + f * jnp.exp2(depth[k * levels : (k + 1) * levels] * scale)
                top = top + f
            return down, top

        down, top = lax.fori_loop(
            0, points // group, body, (jnp.zeros((levels, width), F32), jnp.float32(0.0))
        )
        above = jnp.concatenate([jnp.full((1, width), top, F32), down[:-1]], axis=0)
        value = cos * (above - down)
        for k, b in enumerate(blocks):
            tile = slice(k * BLOCK, (k + 1) * BLOCK)
            on = jnp.where(lit[b] > 0, 1.0, 0.0)
            weight = mass[:, b * BLOCK : (b + 1) * BLOCK].astype(F32)
            out[:, tile] = on * value[:, tile] / weight


def struct(shape, dtype=F32):
    return jax.ShapeDtypeStruct(shape, dtype)


def shards(
    tracers, velocity, metric, absorber, cosine, mass, absorption, flux, lit, neighbour, edge
):
    count, levels, cols = tracers.shape
    gases, points, _ = absorption.shape
    peers = lax.axis_size("sfc")
    total = neighbour.shape[1] * peers
    rows = count * levels
    up = [(i, (i + 1) % peers) for i in range(peers)]
    down = [(j, i) for i, j in up]
    tr = tracers.reshape(rows, cols)
    vel = velocity.reshape(2 * levels, cols)
    metric = metric.reshape(1, cols)
    cosine = cosine.reshape(1, cols)
    chunk = 2 * levels
    side = struct((rows, BLOCK))

    left, right, wide, fine = pl.pallas_call(
        functools.partial(rim_kernel, levels),
        in_specs=[HBM, HBM, VMEM],
        out_specs=[VMEM] * 4,
        out_shape=[side, side, struct((2 * BLOCK, 2 * BLOCK), BF16), struct((BLOCK, 2 * BLOCK), BF16)],
        scratch_shapes=[
            pltpu.VMEM((2, rows, BLOCK), F32),
            pltpu.VMEM((2, 2 * levels, BLOCK), F32),
            pltpu.SemaphoreType.DMA((4,)),
        ],
        compiler_params=params(),
        name="rims_first",
    )(tr, vel, metric)
    from_left = lax.ppermute(right, "sfc", up)
    from_right = lax.ppermute(left, "sfc", down)

    def heat(blocks, name):
        group = 8
        return pl.pallas_call(
            functools.partial(heat_kernel, blocks, group),
            in_specs=[VMEM] * 4 + [SMEM, SMEM],
            out_specs=VMEM,
            out_shape=struct((levels, len(blocks) * BLOCK)),
            scratch_shapes=[
                pltpu.VMEM((points, gases * levels), F32),
                pltpu.VMEM((group * levels, len(blocks) * BLOCK), F32),
            ],
            compiler_params=params(),
            cost_estimate=cost(1e9),
            name=name,
        )(absorber, cosine, mass, absorption, flux, lit)

    part, speed, local, halo = pl.pallas_call(
        functools.partial(first_kernel, total, levels, chunk),
        in_specs=[VMEM] * 9,
        out_specs=[VMEM] * 4,
        out_shape=[
            struct((rows, cols)),
            struct((2 * levels, cols)),
            struct((cols, cols), BF16),
            struct((2 * BLOCK, cols), BF16),
        ],
        compiler_params=params(),
        cost_estimate=cost(1e9),
        name="first_local",
    )(tr, vel, metric, wide, fine, left, right, neighbour, edge)
    heat_rim = heat((0, 3), "heat_rims")

    own_left, own_right = pl.pallas_call(
        functools.partial(rim2_kernel, levels),
        in_specs=[VMEM] * 9,
        out_specs=[VMEM] * 2,
        out_shape=[side, side],
        compiler_params=params(),
        name="rims_second",
    )(part, from_left, from_right, halo, wide, fine, tr, speed, heat_rim)
    next_left = lax.ppermute(own_right, "sfc", up)
    next_right = lax.ppermute(own_left, "sfc", down)
    heat_in = heat((1, 2), "heat_inner")
    part2, heating = pl.pallas_call(
        functools.partial(inner2_kernel, levels, chunk),
        in_specs=[VMEM] * 13,
        out_specs=[VMEM] * 2,
        out_shape=[struct((rows, cols)), struct((levels, cols))],
        compiler_params=params(),
        cost_estimate=cost(1e9),
        name="second_local",
    )(
        part, from_left, from_right, halo, local, wide, fine, tr, speed, heat_rim, heat_in,
        own_left, own_right,
    )
    advanced = pl.pallas_call(
        functools.partial(last_kernel, chunk),
        in_specs=[VMEM] * 4,
        out_specs=VMEM,
        out_shape=struct((rows, cols)),
        compiler_params=params(),
        name="last",
    )(part2, next_left, next_right, halo)
    return advanced.reshape(tracers.shape), heating


def solution(mesh):
    placed = (
        P(None, None, ("grp", "sfc")),
        P(None, None, ("grp", "sfc")),
        P(("grp", "sfc")),
        P(("grp", "sfc"), None),
        P(("grp", "sfc")),
        P(None, ("grp", "sfc")),
        P(),
        P(),
        P(("grp", "sfc")),
        P(None, ("grp", "sfc")),
        P(None, ("grp", "sfc")),
    )
    return jax.shard_map(
        shards,
        mesh=mesh,
        in_specs=placed,
        out_specs=(P(None, None, ("grp", "sfc")), P(None, ("grp", "sfc"))),
        check_vma=False,
    )
```

time: 206 us -> 35.1 us (0.17)
  the two profiles are of different devices: /device:TPU:9 before, /device:TPU:0 now
where the time goes in v1:
time: 35.1 us; the launch traced here: 34.8 us
  Pallas kernels  10.6 us (30%)
  starting transfers between devices  10.5 us (30%)
  waiting for transfers between devices  8.5 us (24%)
  local copies, waits for them, and re-layouts  4.49 us (13%)
  between operations  0.78 us (2%)
    ppermute x1, starting transfers between devices, shards(): from_right = lax.ppermute(left, 'sfc', down)  5.5 us
    ppermute x1, starting transfers between devices, shards(): next_right = lax.ppermute(own_left, 'sfc', down)  4.95 us
    ppermute x1, waiting for transfers between devices, shards(): next_left = lax.ppermute(own_right, 'sfc', up)  4.6 us
    unnamed x25, local copies, waits for them, and re-layouts  4.49 us
    ppermute x1, waiting for transfers between devices, shards(): from_left = lax.ppermute(right, 'sfc', up)  3.67 us
    pallas_call x1, Pallas kernels, shards(): pl.pallas_call(functools.partial(inner2_kernel, levels, chunk), in_specs=...  3.1 us
    pallas_call x1, Pallas kernels, shards(): pl.pallas_call(functools.partial(first_kernel, total, levels, chunk), in_...  2.51 us
    pallas_call x1, Pallas kernels, shards(): pl.pallas_call(functools.partial(last_kernel, chunk), in_specs=[VMEM] * 4...  1.91 us
  transfers between devices with their start and end apart: 4, of which 3 were waited for; matrix products, arithmetic and copies ran while one was open for 3% of the time, Pallas kernels for 19%

profile of v1, /device:TPU:0, one launch (start us, length us, event | category | flops | bytes accessed | tf_op | source)
XLA Modules:
  0.0 34.8 jit_solution(8390185087465594796)
XLA Ops:
  0.6 0.0 copy-start.4
  0.6 0.7 %copy-done.4 = f32[512]{0:T(512)S(1)} copy-done((f32[512]{0:T(512)S(1)}, f32[512]{0:T(512)}, u32[]{:S(2)}) %copy-start.4) | copy-done | bytes 2072
  1.3 1.2 %copy-done = f32[8,64,512]{2,1,0:T(8,128)S(1)} copy-done((f32[8,64,512]{2,1,0:T(8,128)S(1)}, f32[8,64,512]{2,1,0:T(8,128)}, u32[]{:S(2)}) %copy-start) | copy-done | bytes 1048600
  2.5 0.9 %copy-done.2 = f32[2,64,512]{2,1,0:T(8,128)S(1)} copy-done((f32[2,64,512]{2,1,0:T(8,128)S(1)}, f32[2,64,512]{2,1,0:T(8,128)}, u32[]{:S(2)}) %copy-start.2) | copy-done | bytes 262168
  3.5 0.7 %rims_first.1 = (f32[512,128]{1,0:T(8,128)S(1)}, f32[512,128]{1,0:T(8,128)S(1)}, bf16[256,256]{1,0:T(8,128)(2,1)S(1)}, bf16[128,256]{1,0:T(8,128)(2,1)S(1)}) custom-call(f32[512,512]{1,0:T(8,128)S(1)} %bitcast.4, f32[128,512]{1,0:T(8,128)S(1)} %bitcast.8, f32[1,512]{1,0:T(1,128)S(1)} %bitcast.10), custom_call_target="tpu_custom_call" | custom-call | tf_op jit(solution)/shard_map/rims_first/pallas_call | solution.py:296
  4.2 0.0 copy-start.11
  4.3 5.5 %collective-permute-start.1 = (f32[512,128]{1,0:T(8,128)S(1)}, f32[512,128]{1,0:T(8,128)S(1)}, u32[]{:S(2)}, u32[]{:S(2)}) collective-permute-start(f32[512,128]{1,0:T(8,128)S(1)} %get-tuple-element.16.left), channel_id=1, source_target_pairs={{1,0},{2,1},{3,2},{4,3},{5,4},{6,5},{7,6},{8,7},{9,8},{10,9},{11,1... | collective-permute-start | bytes 786440 | tf_op jit(solution)/shard_map/ppermute | solution.py:310
  9.8 0.0 collective-permute-start
  9.8 0.0 copy-start.8
  9.8 1.0 %copy.13.absorption = bf16[4,112,64]{2,1,0:T(8,128)(2,1)S(1)} copy(bf16[4,112,64]{1,2,0:T(8,128)(2,1)} %param.17) | data formatting | bytes 114688 | tf_op args[6]
  10.7 0.0 copy-start.7
  10.8 0.6 %copy-done.7 = s32[4,32]{1,0:T(4,128)S(1)} copy-done((s32[4,32]{1,0:T(4,128)S(1)}, s32[4,32]{1,0:T(4,128)}, u32[]{:S(2)}) %copy-start.7) | copy-done | bytes 536
  11.4 2.5 %first_local.1 = (f32[512,512]{1,0:T(8,128)S(1)}, f32[128,512]{1,0:T(8,128)S(1)}, bf16[512,512]{1,0:T(8,128)(2,1)S(1)}, bf16[256,512]{1,0:T(8,128)(2,1)S(1)}) custom-call(f32[512,512]{1,0:T(8,128)S(1)} %bitcast.5, f32[128,512]{1,0:T(8,128)S(1)} %bitcast.9, f32[1,512]{1,0:T(1,128)S(1)} %bitcast.11, bf16[256,256]{1,0:T(8,128)(2,1)S(1)} %get-tuple-element.14.wide, ...), custom_call_target="tpu_custom_call" | custom-call | flops 1000000000 | bytes 1048576 | tf_op jit(solution)/shard_map/first_local/pallas_call | solution.py:328
  14.0 0.6 %heat_rims.1.heat.heat_rim = f32[64,256]{1,0:T(8,128)S(1)} custom-call(bf16[512,256]{1,0:T(8,128)(2,1)S(1)} %copy-done.5, bf16[1,512]{1,0:T(2,128)(2,1)S(1)} %reshape.22.cosine, bf16[64,512]{1,0:T(8,128)(2,1)S(1)} %copy-done.6, bf16[4,112,64]{2,1,0:T(8,128)(2,1)S(1)} %copy.13.absorption, f32[112]{0:T(128)S(1)} %copy-done.9, s32[4]{0:T(128)S(1)} %copy-done.10), custom_call_target="tpu_custom_call" | custom-call | flops 1000000000 | bytes 1048576 | tf_op jit(solution)/shard_map/heat_rims/pallas_call | solution.py:314
  14.6 0.0 collective-permute-done.1.right
  14.6 3.7 %collective-permute-done.left = f32[512,128]{1,0:T(8,128)S(1)} collective-permute-done((f32[512,128]{1,0:T(8,128)S(1)}, f32[512,128]{1,0:T(8,128)S(1)}, u32[]{:S(2)}, u32[]{:S(2)}) %collective-permute-start) | collective-permute-done | bytes 262176 | tf_op jit(solution)/shard_map/ppermute | solution.py:309
  18.3 1.2 %rims_second.1 = (f32[512,128]{1,0:T(8,128)S(1)}, f32[512,128]{1,0:T(8,128)S(1)}) custom-call(f32[512,512]{1,0:T(8,128)S(1)} %get-tuple-element.18.part, f32[512,128]{1,0:T(8,128)S(1)} %collective-permute-done.left, f32[512,128]{1,0:T(8,128)S(1)} %collective-permute-done.1.right, bf16[256,512]{1,0:T(8,128)(2,1)S(1)} %get-tuple-element.19.halo, ...), custom_call_target="tpu_custom_call" | custom-call | tf_op jit(solution)/shard_map/rims_second/pallas_call | solution.py:344
  19.5 5.0 %collective-permute-start.3 = (f32[512,128]{1,0:T(8,128)S(1)}, f32[512,128]{1,0:T(8,128)S(1)}, u32[]{:S(2)}, u32[]{:S(2)}) collective-permute-start(f32[512,128]{1,0:T(8,128)S(1)} %get-tuple-element.22.own_left), channel_id=1, source_target_pairs={{1,0},{2,1},{3,2},{4,3},{5,4},{6,5},{7,6},{8,7},{9,8},{10,9},{11,1... | collective-permute-start | bytes 786440 | tf_op jit(solution)/shard_map/ppermute | solution.py:353
  24.4 0.0 collective-permute-start.2
  24.4 0.6 %heat_inner.1.heat_in = f32[64,256]{1,0:T(8,128)S(1)} custom-call(bf16[512,256]{1,0:T(8,128)(2,1)S(1)} %copy-done.5, bf16[1,512]{1,0:T(2,128)(2,1)S(1)} %reshape.22.cosine, bf16[64,512]{1,0:T(8,128)(2,1)S(1)} %copy-done.6, bf16[4,112,64]{2,1,0:T(8,128)(2,1)S(1)} %copy.13.absorption, f32[112]{0:T(128)S(1)} %copy-done.9, s32[4]{0:T(128)S(1)} %copy-done.10), custom_call_target="tpu_custom_call" | custom-call | flops 1000000000 | bytes 1048576 | tf_op jit(solution)/shard_map/heat_inner/pallas_call | solution.py:314
  25.0 3.1 %second_local.1 = (f32[512,512]{1,0:T(8,128)S(1)}, f32[64,512]{1,0:T(8,128)}) custom-call(f32[512,512]{1,0:T(8,128)S(1)} %get-tuple-element.18.part, f32[512,128]{1,0:T(8,128)S(1)} %collective-permute-done.left, f32[512,128]{1,0:T(8,128)S(1)} %collective-permute-done.1.right, bf16[256,512]{1,0:T(8,128)(2,1)S(1)} %get-tuple-element.19.halo, ...), custom_call_target="tpu_custom_call" | custom-call | flops 1000000000 | bytes 1048576 | tf_op jit(solution)/shard_map/second_local/pallas_call | solution.py:355
  28.1 0.2 collective-permute-done.3.right
  28.3 4.6 %collective-permute-done.2.left = f32[512,128]{1,0:T(8,128)S(1)} collective-permute-done((f32[512,128]{1,0:T(8,128)S(1)}, f32[512,128]{1,0:T(8,128)S(1)}, u32[]{:S(2)}, u32[]{:S(2)}) %collective-permute-start.2) | collective-permute-done | bytes 262176 | tf_op jit(solution)/shard_map/ppermute | solution.py:352
  32.9 1.9 %last.1 = f32[512,512]{1,0:T(8,128)} custom-call(f32[512,512]{1,0:T(8,128)S(1)} %get-tuple-element.24.part, f32[512,128]{1,0:T(8,128)S(1)} %collective-permute-done.2.left, f32[512,128]{1,0:T(8,128)S(1)} %collective-permute-done.3.right, bf16[256,512]{1,0:T(8,128)(2,1)S(1)} %get-tuple-element.19.halo), custom_call_target="tpu_custom_call" | custom-call | tf_op jit(solution)/shard_map/last/pallas_call | solution.py:367
  (17 shorter events, 0.0 us)
Async XLA Ops:
  0.6 0.7 %copy-start.4 = (f32[512]{0:T(512)S(1)}, f32[512]{0:T(512)}, u32[]{:S(2)}) copy-start(f32[512]{0:T(512)} %param.13) | copy-start | bytes 6148
  1.3 1.2 %copy-start = (f32[8,64,512]{2,1,0:T(8,128)S(1)}, f32[8,64,512]{2,1,0:T(8,128)}, u32[]{:S(2)}) copy-start(f32[8,64,512]{2,1,0:T(8,128)} %param.11) | copy-start | bytes 3145732
  2.5 0.9 %copy-start.2 = (f32[2,64,512]{2,1,0:T(8,128)S(1)}, f32[2,64,512]{2,1,0:T(8,128)}, u32[]{:S(2)}) copy-start(f32[2,64,512]{2,1,0:T(8,128)} %param.12) | copy-start | bytes 786436
  3.5 7.3 %copy-start.1 = (f32[8,64,512]{2,1,0:T(8,128)S(1)}, f32[8,64,512]{2,1,0:T(8,128)}, u32[]{:S(2)}) copy-start(f32[8,64,512]{2,1,0:T(8,128)} %param.11) | copy-start | bytes 3145732
  3.5 7.3 %copy-start.3 = (f32[2,64,512]{2,1,0:T(8,128)S(1)}, f32[2,64,512]{2,1,0:T(8,128)}, u32[]{:S(2)}) copy-start(f32[2,64,512]{2,1,0:T(8,128)} %param.12) | copy-start | bytes 786436
  4.2 5.5 %copy-start.11 = (bf16[512]{0:T(512)(128)(2,1)S(1)}, bf16[512]{0:T(512)(128)(2,1)}, u32[]{:S(2)}) copy-start(bf16[512]{0:T(512)(128)(2,1)} %param.15) | copy-start | bytes 3076
  4.3 10.3 %collective-permute-start.1 = (f32[512,128]{1,0:T(8,128)S(1)}, f32[512,128]{1,0:T(8,128)S(1)}, u32[]{:S(2)}, u32[]{:S(2)}) collective-permute-start(f32[512,128]{1,0:T(8,128)S(1)} %get-tuple-element.16.left), channel_id=1, source_target_pairs={{1,0},{2,1},{3,2},{4,3},{5,4},{6,5},{7,6},{8,7},{9,8},{10,9},{11,1... | collective-permute-start | bytes 786440 | tf_op jit(solution)/shard_map/ppermute | solution.py:310
  9.8 8.5 %collective-permute-start = (f32[512,128]{1,0:T(8,128)S(1)}, f32[512,128]{1,0:T(8,128)S(1)}, u32[]{:S(2)}, u32[]{:S(2)}) collective-permute-start(f32[512,128]{1,0:T(8,128)S(1)} %get-tuple-element.17.right), channel_id=1, source_target_pairs={{0,1},{1,2},{2,3},{3,4},{4,5},{5,6},{6,7},{7,8},{8,9},{9,10},{10,1... | collective-permute-start | bytes 786440 | tf_op jit(solution)/shard_map/ppermute | solution.py:309
  9.8 1.0 %copy-start.8 = (s32[4,32]{1,0:T(4,128)S(1)}, s32[4,32]{1,0:T(4,128)}, u32[]{:S(2)}) copy-start(s32[4,32]{1,0:T(4,128)} %ne.1) | copy-start | bytes 1540
  10.7 0.7 %copy-start.7 = (s32[4,32]{1,0:T(4,128)S(1)}, s32[4,32]{1,0:T(4,128)}, u32[]{:S(2)}) copy-start(s32[4,32]{1,0:T(4,128)} %nb.1) | copy-start | bytes 1540
  11.4 2.5 %copy-start.5 = (bf16[512,256]{1,0:T(8,128)(2,1)S(1)}, bf16[512,256]{1,0:T(8,128)(2,1)}, u32[]{:S(2)}) copy-start(bf16[512,256]{1,0:T(8,128)(2,1)} %absorber.3) | copy-start | bytes 786436
  11.4 2.5 %copy-start.6 = (bf16[64,512]{1,0:T(8,128)(2,1)S(1)}, bf16[64,512]{1,0:T(8,128)(2,1)}, u32[]{:S(2)}) copy-start(bf16[64,512]{1,0:T(8,128)(2,1)} %mass.3) | copy-start | bytes 196612
  11.4 2.6 %copy-start.9 = (f32[112]{0:T(128)S(1)}, f32[112]{0:T(128)}, u32[]{:S(2)}) copy-start(f32[112]{0:T(128)} %flux.3) | copy-start | bytes 1348
  11.4 2.6 %copy-start.10 = (s32[4]{0:T(128)S(1)}, s32[4]{0:T(128)}, u32[]{:S(2)}) copy-start(s32[4]{0:T(128)} %lit.3) | copy-start | bytes 52
  19.5 8.8 %collective-permute-start.3 = (f32[512,128]{1,0:T(8,128)S(1)}, f32[512,128]{1,0:T(8,128)S(1)}, u32[]{:S(2)}, u32[]{:S(2)}) collective-permute-start(f32[512,128]{1,0:T(8,128)S(1)} %get-tuple-element.22.own_left), channel_id=1, source_target_pairs={{1,0},{2,1},{3,2},{4,3},{5,4},{6,5},{7,6},{8,7},{9,8},{10,9},{11,1... | collective-permute-start | bytes 786440 | tf_op jit(solution)/shard_map/ppermute | solution.py:353
  24.4 8.5 %collective-permute-start.2 = (f32[512,128]{1,0:T(8,128)S(1)}, f32[512,128]{1,0:T(8,128)S(1)}, u32[]{:S(2)}, u32[]{:S(2)}) collective-permute-start(f32[512,128]{1,0:T(8,128)S(1)} %get-tuple-element.23.own_right), channel_id=1, source_target_pairs={{0,1},{1,2},{2,3},{3,4},{4,5},{5,6},{6,7},{7,8},{8,9},{9,10},{10,1... | collective-permute-start | bytes 786440 | tf_op jit(solution)/shard_map/ppermute | solution.py:352

commit v2 on v1

v2 whole, which is shorter than its diff:
```python
import functools
import math

import jax
import jax.numpy as jnp
import numpy as np
from jax import lax
from jax.experimental import pallas as pl
from jax.experimental.pallas import tpu as pltpu
from jax.sharding import PartitionSpec as P

BLOCK = 128
RIM = 8
STEP = 0.1
F32 = jnp.float32
BF16 = jnp.bfloat16
VMEM = pl.BlockSpec(memory_space=pltpu.VMEM)
SMEM = pl.BlockSpec(memory_space=pltpu.SMEM)
HBM = pl.BlockSpec(memory_space=pltpu.HBM)


def derivative_table():
    nodes = np.array([-1.0, -1.0 / math.sqrt(5.0), 1.0 / math.sqrt(5.0), 1.0])
    weights = np.array(
        [1.0 / np.prod([nodes[i] - nodes[m] for m in range(4) if m != i]) for i in range(4)]
    )
    table = np.zeros((4, 4))
    for i in range(4):
        for m in range(4):
            if i != m:
                table[i, m] = weights[m] / weights[i] / (nodes[i] - nodes[m])
        table[i, i] = -sum(table[i, m] for m in range(4) if m != i)
    return table


def params(mib=8):
    return pltpu.CompilerParams(vmem_limit_bytes=mib << 20)


def cost(flops, size=1 << 20):
    return pl.CostEstimate(flops=int(flops), bytes_accessed=int(size), transcendentals=0)


def iota(shape, dim):
    return lax.broadcasted_iota(jnp.int32, shape, dim)


def split(x):
    high = x.astype(BF16)
    return high, (x - high.astype(F32)).astype(BF16)


def dot(a, b):
    return jnp.dot(a, b, preferred_element_type=F32)


def build_derivatives(wide_ref, fine_ref):
    table = derivative_table()
    src, dst = iota((BLOCK, BLOCK), 0), iota((BLOCK, BLOCK), 1)
    si, sj, di, dj = src // 4 % 4, src % 4, dst // 4 % 4, dst % 4
    same = src // 16 == dst // 16
    halves = []
    for d, s, keep in ((di, si, same & (sj == dj)), (dj, sj, same & (si == di))):
        pick = jnp.where(keep, d * 4 + s, -1)
        value = jnp.zeros((BLOCK, BLOCK), F32)
        for i in range(4):
            for m in range(4):
                value = jnp.where(pick == i * 4 + m, float(table[i, m]), value)
        halves.append(value)
    high, low = split(jnp.concatenate(halves, axis=1))
    wide_ref[:BLOCK] = high
    wide_ref[BLOCK:] = high
    fine_ref[...] = low


def advance(field, first, second, wide_ref, fine_ref):
    high, low = split(field)
    both = dot(jnp.concatenate([high, low], axis=1), wide_ref[...]) + dot(high, fine_ref[...])
    return field + first * both[:, :BLOCK] + second * both[:, BLOCK:]


def repeat_rows(x, times):
    return jnp.concatenate([x] * times, axis=0) if times > 1 else x


def rim_starts(cols):
    near = jnp.where(lax.axis_index("sfc") % 2 == 0, cols - BLOCK, 0)
    return pl.multiple_of(near, BLOCK), pl.multiple_of(cols - BLOCK - near, BLOCK)


def rim_kernel(levels, *refs):
    count = (len(refs) - 5) // 2
    given, (near, far, wide, fine), kept, sems = (
        refs[:count], refs[count : count + 4], refs[count + 4 : -1], refs[-1],
    )
    tr_hbm, vel_hbm, metric_hbm = given[:3]
    tr, vel, metric = kept[:3]
    rows, cols = tr.shape
    rims = (pl.ds(0, BLOCK), pl.ds(cols - BLOCK, BLOCK))
    inner = pl.ds(BLOCK, cols - 2 * BLOCK)
    pairs = [(metric_hbm, metric)]
    pairs += [(hbm.at[:, r], ref.at[:, r]) for r in rims for hbm, ref in ((vel_hbm, vel), (tr_hbm, tr))]
    pairs += [(hbm.at[:, inner], ref.at[:, inner]) for hbm, ref in ((vel_hbm, vel), (tr_hbm, tr))]
    pairs += list(zip(given[3:], kept[3:], strict=True))
    copies = [pltpu.make_async_copy(a, b, sems.at[k]) for k, (a, b) in enumerate(pairs)]
    for copy in copies:
        copy.start()
    build_derivatives(wide, fine)
    copies[0].wait()
    for copy in copies[1:5]:
        copy.wait()
    for start, out in zip(rim_starts(cols), (near, far), strict=True):
        rim = pl.ds(start, BLOCK)
        scale = -STEP * metric[:, rim]
        first = repeat_rows(vel[:levels, rim] * scale, rows // levels)
        second = repeat_rows(vel[levels:, rim] * scale, rows // levels)
        out[...] = advance(tr[:, rim], first, second, wide, fine)
    for copy in copies[5:]:
        copy.wait()


def build_assembly(total, position, nb, ne, local, halo):
    elems, cols = nb.shape[1], local.shape[1]
    index = nb[...] - position * elems + RIM
    index = jnp.where(index < 0, index + total, index)
    index = jnp.where(index >= total, index - total, index)
    code = (index * 4 + ne[...]).astype(F32).astype(BF16)
    spread = (iota((elems, cols), 1) // 16 == iota((elems, cols), 0)).astype(F32).astype(BF16)
    code = dot(code, spread).astype(jnp.int32)
    lane = iota((1, cols), 1)
    i, j = lane // 4 % 4, lane % 4

    def source(code, p):
        edge, q = code % 4, 3 - p
        si = jnp.where(edge == 0, 0, jnp.where(edge == 1, q, jnp.where(edge == 2, 3, 3 - q)))
        sj = jnp.where(edge == 0, q, jnp.where(edge == 1, 3, jnp.where(edge == 2, 3 - q, 0)))
        return code // 4 * 16 + si * 4 + sj

    across = jnp.where(i == 0, source(code[0:1], j), source(code[2:3], 3 - j))
    across = jnp.where((i == 0) | (i == 3), across, -1)
    along = jnp.where(j == 3, source(code[1:2], i), source(code[3:4], 3 - i))
    along = jnp.where((j == 0) | (j == 3), along, -1)
    own = 1.0 - 0.5 * ((across >= 0).astype(F32) + (along >= 0).astype(F32))

    def rows_of(start):
        row = iota((BLOCK, cols), 0) + start
        return jnp.where(row == across, 0.5, 0.0) + jnp.where(row == along, 0.5, 0.0)

    even = position % 2 == 0
    halo[:BLOCK] = rows_of(jnp.where(even, BLOCK + cols, 0)).astype(BF16)
    halo[BLOCK:] = rows_of(jnp.where(even, 0, BLOCK + cols)).astype(BF16)
    for r in range(0, cols, BLOCK):
        value = rows_of(BLOCK + r) + jnp.where(iota((BLOCK, cols), 0) + r == lane, own, 0.0)
        local[r : r + BLOCK] = value.astype(BF16)


def first_kernel(
    total, levels, tr, vel, metric, wide, fine, near, far, nb, ne,
    part, speed, local, halo, high, low,
):
    rows, cols = tr.shape
    scale = -STEP * metric[...]
    speed[...] = vel[...] * scale
    for b in range(BLOCK, cols - BLOCK, BLOCK):
        tile = slice(b, b + BLOCK)
        first = repeat_rows(speed[:levels, tile], rows // levels)
        second = repeat_rows(speed[levels:, tile], rows // levels)
        high[:, tile], low[:, tile] = split(advance(tr[:, tile], first, second, wide, fine))
    for start, value in zip(rim_starts(cols), (near, far), strict=True):
        tile = pl.ds(start, BLOCK)
        high[:, tile], low[:, tile] = split(value[...])
    build_assembly(total, lax.axis_index("sfc"), nb, ne, local, halo)
    part[...] = dot(high[...], local[...]) + dot(low[...], local[...])


def halo_parts(near, far):
    nh, nl = split(near)
    fh, fl = split(far)
    return jnp.concatenate([nh, fh], axis=1), jnp.concatenate([nl, fl], axis=1)


def rim2_kernel(
    levels, part, near, far, halo, wide, fine, tr, speed, heat, out_near, out_far, high, low
):
    rows, cols = part.shape
    high[...], low[...] = halo_parts(near[...], far[...])
    for start, out in zip(rim_starts(cols), (out_near, out_far), strict=True):
        tile = pl.ds(start, BLOCK)
        warm_tile = pl.ds(pl.multiple_of(jnp.where(start == 0, 0, BLOCK), BLOCK), BLOCK)
        section = part[:, tile] + dot(high[...], halo[:, tile]) + dot(low[...], halo[:, tile])
        first = repeat_rows(speed[:levels, tile], rows // levels)
        second = repeat_rows(speed[levels:, tile], rows // levels)
        field = 0.5 * (tr[:, tile] + advance(section, first, second, wide, fine))
        warm = (0.5 * STEP) * heat[:, warm_tile]
        out[:levels] = field[:levels] + warm
        out[levels:] = field[levels:]


def inner2_kernel(
    levels, part, high, low, halo, local, wide, fine, tr, speed, heat,
    own_near, own_far, out, own_high, own_low,
):
    rows, cols = part.shape
    inner = slice(BLOCK, cols - BLOCK)
    section = part[:, inner] + dot(high[...], halo[:, inner]) + dot(low[...], halo[:, inner])
    for b in range(BLOCK, cols - BLOCK, BLOCK):
        tile = slice(b, b + BLOCK)
        first = repeat_rows(speed[:levels, tile], rows // levels)
        second = repeat_rows(speed[levels:, tile], rows // levels)
        field = advance(section[:, b - BLOCK : b], first, second, wide, fine)
        field = 0.5 * (tr[:, tile] + field)
        warm = (0.5 * STEP) * heat[:, b - BLOCK : b]
        field = jnp.concatenate([field[:levels] + warm, field[levels:]], axis=0)
        own_high[:, tile], own_low[:, tile] = split(field)
    for start, value in zip(rim_starts(cols), (own_near, own_far), strict=True):
        tile = pl.ds(start, BLOCK)
        own_high[:, tile], own_low[:, tile] = split(value[...])
    out[...] = dot(own_high[...], local[...]) + dot(own_low[...], local[...])


def last_kernel(chunk, part, near, far, halo, heat_rim, heat_in, out_hbm, heat_hbm, out, sems):
    rows, cols = part.shape
    pairs = [
        (heat_rim.at[:, pl.ds(0, BLOCK)], heat_hbm.at[:, pl.ds(0, BLOCK)]),
        (heat_in, heat_hbm.at[:, pl.ds(BLOCK, cols - 2 * BLOCK)]),
        (heat_rim.at[:, pl.ds(BLOCK, BLOCK)], heat_hbm.at[:, pl.ds(cols - BLOCK, BLOCK)]),
    ]
    copies = [pltpu.make_async_copy(a, b, sems.at[k]) for k, (a, b) in enumerate(pairs)]
    for copy in copies:
        copy.start()
    for k, r0 in enumerate(range(0, rows, chunk)):
        r = pl.ds(r0, chunk)
        high, low = halo_parts(near[r], far[r])
        out[r] = part[r] + dot(high, halo[...]) + dot(low, halo[...])
        copy = pltpu.make_async_copy(out.at[r], out_hbm.at[r], sems.at[len(pairs) + k])
        copy.start()
        copies.append(copy)
    for copy in copies:
        copy.wait()


def heat_kernel(blocks, build, after, absorber, cosine, mass, absorption, flux, lit, *refs):
    if build:
        out, weights, depth, beams = refs
    else:
        weights, out, depth, beams = refs
    gases, levels, points = absorption.shape
    width = len(blocks) * BLOCK
    span = gases * levels

    if build:

        @pl.when(jnp.max(lit[...]) > 0)
        def _():
            table = absorption[...].astype(F32).reshape(span, points).T
            keep = iota((levels, span), 1) % levels <= iota((levels, span), 0)
            for g in range(points):
                weights[g * levels : (g + 1) * levels] = jnp.where(keep, table[g : g + 1], 0.0).astype(BF16)

    lanes = iota(lit.shape, 1)
    chosen = functools.reduce(jnp.logical_or, [lanes == b for b in blocks])
    any_lit = jnp.max(jnp.where(chosen, lit[...], 0))

    @pl.when(any_lit == 0)
    def _():
        out[...] = jnp.zeros_like(out)

    @pl.when(any_lit > 0)
    def _():
        beams[...] = jnp.broadcast_to(jnp.broadcast_to(flux[...], (8, points)).T[:, :1], beams.shape)
        amounts = jnp.concatenate([absorber[b * BLOCK : (b + 1) * BLOCK] for b in blocks], axis=0)
        cos = jnp.concatenate([cosine[:, b * BLOCK : (b + 1) * BLOCK] for b in blocks], axis=1)
        cos = cos.astype(F32)
        scale = jnp.broadcast_to(-math.log2(math.e) / cos, (8, width))
        depth[...] = dot(weights[...], amounts.T)
        strips = []
        for r in range(0, levels, 8):
            tiles = []
            for t in range(0, width, BLOCK):
                total = jnp.zeros((8, BLOCK), F32)
                for g in range(points):
                    d = depth[g * levels + r : g * levels + r + 8, t : t + BLOCK]
                    total = total + beams[g : g + 1] * jnp.exp2(d * scale[:, t : t + BLOCK])
                tiles.append(total)
            strips.append(jnp.concatenate(tiles, axis=1))
        down = jnp.concatenate(strips, axis=0)
        top = jnp.sum(beams[...], axis=0, keepdims=True)
        top = jnp.concatenate([top] * len(blocks), axis=1)
        above = jnp.concatenate([top, down[:-1]], axis=0)
        value = cos * (above - down)
        for k, b in enumerate(blocks):
            tile = slice(k * BLOCK, (k + 1) * BLOCK)
            on = jnp.max(jnp.where(lanes == b, lit[...], 0)).astype(F32)
            weight = mass[:, b * BLOCK : (b + 1) * BLOCK].astype(F32)
            out[:, tile] = on * value[:, tile] / weight


def struct(shape, dtype=F32):
    return pltpu.VMEM(shape, dtype)


def shards(
    tracers, velocity, metric, absorber, cosine, mass, absorption, flux, lit, neighbour, edge
):
    count, levels, cols = tracers.shape
    gases, points, _ = absorption.shape
    peers = lax.axis_size("sfc")
    total = neighbour.shape[1] * peers
    rows = count * levels
    pair = [(i, i ^ 1) for i in range(peers)]
    cross = [(i, (i + 2 * (i % 2) - 1) % peers) for i in range(peers)]
    tr = tracers.reshape(rows, cols)
    vel = velocity.reshape(2 * levels, cols)
    metric = metric.reshape(1, cols)
    absorption = absorption.transpose(0, 2, 1)
    flux = flux.reshape(1, points)
    lit = lit.reshape(1, -1)
    side = struct((rows, BLOCK))
    half = struct((rows, 2 * BLOCK), BF16)
    full = struct((rows, cols))

    def like(x):
        return struct(x.shape, x.dtype)

    moved = (tr, vel, metric, neighbour, edge, absorber, mass, absorption, flux, lit, cosine)
    near, far, wide, fine, *moved = pl.pallas_call(
        functools.partial(rim_kernel, levels),
        in_specs=[HBM] * len(moved),
        out_specs=[VMEM] * (4 + len(moved)),
        out_shape=[side, side, struct((2 * BLOCK, 2 * BLOCK), BF16), struct((BLOCK, 2 * BLOCK), BF16)]
        + [like(x) for x in moved],
        scratch_shapes=[pltpu.SemaphoreType.DMA((len(moved) + 4,))],
        compiler_params=params(),
        name="rims_first",
    )(*[pltpu.with_memory_space_constraint(x, pltpu.HBM) for x in moved])
    tr, vel, metric, neighbour, edge, absorber, mass, absorption, flux, lit, cosine = moved
    cosine = cosine.reshape(1, cols)
    from_far = lax.ppermute(far, "sfc", cross)
    from_near = lax.ppermute(near, "sfc", pair)

    weights = struct((points * levels, gases * levels), BF16)

    def heat(after, blocks, name, *extra):
        out = struct((levels, len(blocks) * BLOCK))
        return pl.pallas_call(
            functools.partial(heat_kernel, blocks, not extra),
            in_specs=[HBM] + [VMEM] * (6 + len(extra)),
            out_specs=VMEM if extra else [VMEM] * 2,
            out_shape=out if extra else [out, weights],
            scratch_shapes=[
                pltpu.VMEM((points * levels, len(blocks) * BLOCK), F32),
                pltpu.VMEM((points, BLOCK), F32),
            ],
            compiler_params=params(16),
            cost_estimate=cost(1e9),
            name=name,
        )(after, absorber, cosine, mass, absorption, flux, lit, *extra)

    part, speed, local, halo = pl.pallas_call(
        functools.partial(first_kernel, total, levels),
        in_specs=[VMEM] * 9,
        out_specs=[VMEM] * 4,
        out_shape=[
            full,
            struct((2 * levels, cols)),
            struct((cols, cols), BF16),
            struct((2 * BLOCK, cols), BF16),
        ],
        scratch_shapes=[pltpu.VMEM((rows, cols), BF16)] * 2,
        compiler_params=params(),
        cost_estimate=cost(1e9),
        name="first_local",
    )(tr, vel, metric, wide, fine, near, far, neighbour, edge)
    heat_rim, weights = heat(halo, (0, 3), "heat_rims")

    own_near, own_far, high, low = pl.pallas_call(
        functools.partial(rim2_kernel, levels),
        in_specs=[VMEM] * 9,
        out_specs=[VMEM] * 4,
        out_shape=[side, side, half, half],
        compiler_params=params(),
        name="rims_second",
    )(part, from_near, from_far, halo, wide, fine, tr, speed, heat_rim)
    next_far = lax.ppermute(own_far, "sfc", cross)
    next_near = lax.ppermute(own_near, "sfc", pair)
    heat_in = heat(high, (1, 2), "heat_inner", weights)
    part2 = pl.pallas_call(
        functools.partial(inner2_kernel, levels),
        in_specs=[VMEM] * 12,
        out_specs=VMEM,
        out_shape=full,
        scratch_shapes=[pltpu.VMEM((rows, cols), BF16)] * 2,
        compiler_params=params(),
        cost_estimate=cost(1e9),
        name="second_local",
    )(part, high, low, halo, local, wide, fine, tr, speed, heat_in, own_near, own_far)
    advanced, heating = pl.pallas_call(
        functools.partial(last_kernel, 2 * levels),
        in_specs=[VMEM] * 6,
        out_specs=[HBM] * 2,
        out_shape=[jax.ShapeDtypeStruct((rows, cols), F32), jax.ShapeDtypeStruct((levels, cols), F32)],
        scratch_shapes=[pltpu.VMEM((rows, cols), F32), pltpu.SemaphoreType.DMA((3 + count // 2,))],
        compiler_params=params(),
        name="last",
    )(part2, next_near, next_far, halo, heat_rim, heat_in)
    return advanced.reshape(tracers.shape), heating


def solution(mesh):
    placed = (
        P(None, None, ("grp", "sfc")),
        P(None, None, ("grp", "sfc")),
        P(("grp", "sfc")),
        P(("grp", "sfc"), None),
        P(("grp", "sfc")),
        P(None, ("grp", "sfc")),
        P(),
        P(),
        P(("grp", "sfc")),
        P(None, ("grp", "sfc")),
        P(None, ("grp", "sfc")),
    )
    return jax.shard_map(
        shards,
        mesh=mesh,
        in_specs=placed,
        out_specs=(P(None, None, ("grp", "sfc")), P(None, ("grp", "sfc"))),
        check_vma=False,
    )
```

time: 35.1 us -> 24 us (0.68)
  local copies, waits for them, and re-layouts: 4.49 us -> 0.01 us
  waiting for transfers between devices: 8.5 us -> 4.41 us
  Pallas kernels: 10.6 us -> 8.03 us
    unnamed x25 -> x0, local copies, waits for them, and re-layouts: 4.49 us -> none
    ppermute x4, waiting for transfers between devices: 8.5 us -> 4.41 us  [the longest x1 2.33 us: shards(): next_far = lax.ppermute(own_far, 'sfc', cross)]
    pallas_call x6, Pallas kernels: 9.39 us -> 6.79 us  [the longest x1 1.7 us: shards(): pl.pallas_call(functools.partial(rim_kernel, levels), in_specs=[HBM] * le...]
  transfers between devices with their start and end apart: 4 -> 4, of which waited for: 3 -> 2; matrix products, arithmetic and copies ran while one was open for 3% -> 0% of each run, Pallas kernels for 19% -> 16%
where the time goes in v2:
time: 24 us; the launch traced here: 23.9 us
  starting transfers between devices  10.7 us (45%)
  Pallas kernels  8.03 us (33%)
  waiting for transfers between devices  4.41 us (18%)
  between operations  0.7 us (3%)
    ppermute x1, starting transfers between devices, shards(): from_far = lax.ppermute(far, 'sfc', cross)  5.67 us
    ppermute x1, starting transfers between devices, shards(): next_far = lax.ppermute(own_far, 'sfc', cross)  4.46 us
    ppermute x1, waiting for transfers between devices, shards(): next_far = lax.ppermute(own_far, 'sfc', cross)  2.33 us
    ppermute x1, waiting for transfers between devices, shards(): from_far = lax.ppermute(far, 'sfc', cross)  2.08 us
    pallas_call x1, Pallas kernels, shards(): pl.pallas_call(functools.partial(rim_kernel, levels), in_specs=[HBM] * le...  1.7 us
    pallas_call x1, Pallas kernels, shards(): pl.pallas_call(functools.partial(inner2_kernel, levels), in_specs=[VMEM]...  1.64 us
    pallas_call x1, Pallas kernels, shards(): pl.pallas_call(functools.partial(first_kernel, total, levels), in_specs=[...  1.56 us
    pallas_call x1, Pallas kernels, shards(): pl.pallas_call(functools.partial(last_kernel, 2 * levels), in_specs=[VMEM...  1.27 us
  transfers between devices with their start and end apart: 4, of which 2 were waited for; matrix products, arithmetic and copies ran while one was open for 0% of the time, Pallas kernels for 16%

profile of v2, /device:TPU:0, one launch (start us, length us, event | category | flops | bytes accessed | tf_op | source)
XLA Modules:
  0.0 23.9 jit_solution(8097742706360080816)
XLA Ops:
  0.6 1.7 %rims_first.1 = (f32[512,128]{1,0:T(8,128)S(1)}, f32[512,128]{1,0:T(8,128)S(1)}, bf16[256,256]{1,0:T(8,128)(2,1)S(1)}, bf16[128,256]{1,0:T(8,128)(2,1)S(1)}, f32...) custom-call(f32[512,512]{1,0:T(8,128)} %bitcast.7, ...), custom_call_target="tpu_custom_call" | custom-call | tf_op jit(solution)/shard_map/rims_first/pallas_call | solution.py:326
  2.3 0.5 %collective-permute-start = (f32[512,128]{1,0:T(8,128)S(1)}, f32[512,128]{1,0:T(8,128)S(1)}, u32[]{:S(2)}, u32[]{:S(2)}) collective-permute-start(f32[512,128]{1,0:T(8,128)S(1)} %get-tuple-element.34.near), channel_id=1, source_target_pairs={{0,1},{1,0},{2,3},{3,2},{4,5},{5,4},{6,7},{7,6},{8,9},{9,8},{10,11... | collective-permute-start | bytes 786440 | tf_op jit(solution)/shard_map/ppermute | solution.py:339
  2.9 5.7 %collective-permute-start.1 = (f32[512,128]{1,0:T(8,128)S(1)}, f32[512,128]{1,0:T(8,128)S(1)}, u32[]{:S(2)}, u32[]{:S(2)}) collective-permute-start(f32[512,128]{1,0:T(8,128)S(1)} %get-tuple-element.35.far), channel_id=1, source_target_pairs={{0,15},{1,2},{2,1},{3,4},{4,3},{5,6},{6,5},{7,8},{8,7},{9,10},{10,... | collective-permute-start | bytes 786440 | tf_op jit(solution)/shard_map/ppermute | solution.py:338
  8.5 1.6 %first_local.1 = (f32[512,512]{1,0:T(8,128)S(1)}, f32[128,512]{1,0:T(8,128)S(1)}, bf16[512,512]{1,0:T(8,128)(2,1)S(1)}, bf16[256,512]{1,0:T(8,128)(2,1)S(1)}) custom-call(f32[512,512]{1,0:T(8,128)S(1)} %get-tuple-element.29.tr, f32[128,512]{1,0:T(8,128)S(1)} %get-tuple-element.30.vel, f32[1,512]{1,0:T(1,128)S(1)} %get-tuple-element.31.metric, ...), custom_call_target="tpu_custom_call" | custom-call | flops 1000000000 | bytes 1048576 | tf_op jit(solution)/shard_map/first_local/pallas_call | solution.py:359
  10.1 0.4 %heat_rims.1 = (f32[64,256]{1,0:T(8,128)S(1)}, bf16[7168,256]{1,0:T(8,128)(2,1)S(1)}) custom-call(bf16[256,512]{1,0:T(8,128)(2,1)S(1)} %get-tuple-element.39.after.halo, bf16[512,256]{1,0:T(8,128)(2,1)S(1)} %get-tuple-element.41.absorber, bf16[1,512]{1,0:T(2,128)(2,1)S(1)} %reshape.30.cosine, bf16[64,512]{1,0:T(8,128)(2,1)S(1)} %get-tuple-element.43.mass, ...), custom_call_target="tpu_custom_call" | custom-call | flops 1000000000 | bytes 1048576 | tf_op jit(solution)/shard_map/heat_rims/pallas_call | solution.py:345
  10.5 0.0 collective-permute-done.near
  10.5 2.1 %collective-permute-done.1.far = f32[512,128]{1,0:T(8,128)S(1)} collective-permute-done((f32[512,128]{1,0:T(8,128)S(1)}, f32[512,128]{1,0:T(8,128)S(1)}, u32[]{:S(2)}, u32[]{:S(2)}) %collective-permute-start.1) | collective-permute-done | bytes 262176 | tf_op jit(solution)/shard_map/ppermute | solution.py:338
  12.6 1.2 %rims_second.1 = (f32[512,128]{1,0:T(8,128)S(1)}, f32[512,128]{1,0:T(8,128)S(1)}, bf16[512,256]{1,0:T(8,128)(2,1)S(1)}, bf16[512,256]{1,0:T(8,128)(2,1)S(1)}) custom-call(f32[512,512]{1,0:T(8,128)S(1)} %get-tuple-element.38.part, f32[512,128]{1,0:T(8,128)S(1)} %collective-permute-done.near, f32[512,128]{1,0:T(8,128)S(1)} %collective-permute-done.1.far, ...), custom_call_target="tpu_custom_call" | custom-call | tf_op jit(solution)/shard_map/rims_second/pallas_call | solution.py:376
  13.9 0.1 collective-permute-start.2
  13.9 4.5 %collective-permute-start.3 = (f32[512,128]{1,0:T(8,128)S(1)}, f32[512,128]{1,0:T(8,128)S(1)}, u32[]{:S(2)}, u32[]{:S(2)}) collective-permute-start(f32[512,128]{1,0:T(8,128)S(1)} %get-tuple-element.53.own_far), channel_id=1, source_target_pairs={{0,15},{1,2},{2,1},{3,4},{4,3},{5,6},{6,5},{7,8},{8,7},{9,10},{10,... | collective-permute-start | bytes 786440 | tf_op jit(solution)/shard_map/ppermute | solution.py:384
  18.4 0.2 heat_inner.1.heat.heat_in
  18.6 1.6 %second_local.1.part = f32[512,512]{1,0:T(8,128)S(1)} custom-call(f32[512,512]{1,0:T(8,128)S(1)} %get-tuple-element.38.part, bf16[512,256]{1,0:T(8,128)(2,1)S(1)} %get-tuple-element.48.after.high, bf16[512,256]{1,0:T(8,128)(2,1)S(1)} %get-tuple-element.49.low, bf16[256,512]{1,0:T(8,128)(2,1)S(1)} %get-tuple-element.39.after.halo, ...), custom_call_target="tpu_custom_call" | custom-call | flops 1000000000 | bytes 1048576 | tf_op jit(solution)/shard_map/second_local/pallas_call | solution.py:387
  20.3 0.0 collective-permute-done.2.near
  20.3 2.3 %collective-permute-done.3.far = f32[512,128]{1,0:T(8,128)S(1)} collective-permute-done((f32[512,128]{1,0:T(8,128)S(1)}, f32[512,128]{1,0:T(8,128)S(1)}, u32[]{:S(2)}, u32[]{:S(2)}) %collective-permute-start.3) | collective-permute-done | bytes 262176 | tf_op jit(solution)/shard_map/ppermute | solution.py:384
  22.6 1.3 %last.1 = (f32[512,512]{1,0:T(8,128)}, f32[64,512]{1,0:T(8,128)}) custom-call(f32[512,512]{1,0:T(8,128)S(1)} %second_local.1.part, f32[512,128]{1,0:T(8,128)S(1)} %collective-permute-done.2.near, f32[512,128]{1,0:T(8,128)S(1)} %collective-permute-done.3.far, bf16[256,512]{1,0:T(8,128)(2,1)S(1)} %get-tuple-element.39.after.halo, ...), custom_call_target="tpu_custom_call" | custom-call | tf_op jit(solution)/shard_map/last/pallas_call | solution.py:397
  (1 shorter events, 0.0 us)
Async XLA Ops:
  2.3 8.2 %collective-permute-start = (f32[512,128]{1,0:T(8,128)S(1)}, f32[512,128]{1,0:T(8,128)S(1)}, u32[]{:S(2)}, u32[]{:S(2)}) collective-permute-start(f32[512,128]{1,0:T(8,128)S(1)} %get-tuple-element.34.near), channel_id=1, source_target_pairs={{0,1},{1,0},{2,3},{3,2},{4,5},{5,4},{6,7},{7,6},{8,9},{9,8},{10,11... | collective-permute-start | bytes 786440 | tf_op jit(solution)/shard_map/ppermute | solution.py:339
  2.9 9.8 %collective-permute-start.1 = (f32[512,128]{1,0:T(8,128)S(1)}, f32[512,128]{1,0:T(8,128)S(1)}, u32[]{:S(2)}, u32[]{:S(2)}) collective-permute-start(f32[512,128]{1,0:T(8,128)S(1)} %get-tuple-element.35.far), channel_id=1, source_target_pairs={{0,15},{1,2},{2,1},{3,4},{4,3},{5,6},{6,5},{7,8},{8,7},{9,10},{10,... | collective-permute-start | bytes 786440 | tf_op jit(solution)/shard_map/ppermute | solution.py:338
  13.9 6.4 %collective-permute-start.2 = (f32[512,128]{1,0:T(8,128)S(1)}, f32[512,128]{1,0:T(8,128)S(1)}, u32[]{:S(2)}, u32[]{:S(2)}) collective-permute-start(f32[512,128]{1,0:T(8,128)S(1)} %get-tuple-element.52.own_near), channel_id=1, source_target_pairs={{0,1},{1,0},{2,3},{3,2},{4,5},{5,4},{6,7},{7,6},{8,9},{9,8},{10,11... | collective-permute-start | bytes 786440 | tf_op jit(solution)/shard_map/ppermute | solution.py:385
  13.9 8.7 %collective-permute-start.3 = (f32[512,128]{1,0:T(8,128)S(1)}, f32[512,128]{1,0:T(8,128)S(1)}, u32[]{:S(2)}, u32[]{:S(2)}) collective-permute-start(f32[512,128]{1,0:T(8,128)S(1)} %get-tuple-element.53.own_far), channel_id=1, source_target_pairs={{0,15},{1,2},{2,1},{3,4},{4,3},{5,6},{6,5},{7,8},{8,7},{9,10},{10,... | collective-permute-start | bytes 786440 | tf_op jit(solution)/shard_map/ppermute | solution.py:384
